TPU v7x, 32 devices: a whole 2x2x4 slice. The times are simulated.
32 devices in a mesh: node: 4 (over x, core), rep: 8 (over z, y).
Axes of the slice: x: 2, y: 2, z: 4, core: 2. Of those that a mesh axis runs over, the one named last changes fastest.
Arguments:
- features: bfloat16 [1024, 512], P(('node', 'rep')), may hold values from -6 to 6
- adj_tiles: bfloat16 [8, 4, 6, 128, 128], P('rep', 'node'), may hold values from 0 to 0.024902344
- tile_col: int32 [8, 4, 6], P('rep', 'node'), may hold values from 0 to 1
- tile_count: int32 [8, 4], P('rep', 'node'), may hold values from 1 to 6, as said below
- weight: bfloat16 [512, 512], replicated, may hold values from -0.25 to 0.25
- bias: float32 [512], replicated, may hold values from -3 to 3
- out_grad: bfloat16 [8, 128, 512], P('rep', 'node'), may hold values from -6 to 6
Outputs:
- node_out: bfloat16 [8, 128, 512], P('rep', 'node')
- weight_grad: float32 [512, 512], P('rep')
- input_grad: bfloat16 [1024, 512], P(('node', 'rep'))
Inputs may be any that keep to these rules, and one draw needn't show every extreme that they name: `tile_col`: slot k of block row b and part s names a column block of part s; slots at or after tile_count[b, s] are padding and their tiles and columns are not part of A. `tile_count`: the number of live slots of block row b in part s; the most is reached in every draw.
All inputs are finite; a program needn't handle non-finite values.
Results may differ from a plain program's by a relative error of at most 0.014.
Values may be sent and summed in bfloat16 or wider, within the bound.
A program may use at most 64 MiB of HBM per device.

v0:
```python
import jax
import jax.numpy as jnp
from jax import lax
from jax.sharding import PartitionSpec as P


def on_device(features, adj_tiles, tile_col, tile_count, weight, bias, out_grad):
    rows_dev, hidden_width = features.shape
    node_parts = lax.axis_size("node")
    rep_size = lax.axis_size("rep")
    tile_size = adj_tiles.shape[-1]
    slot_count = adj_tiles.shape[2]
    adj_set = adj_tiles[:, 0]
    tile_cols = tile_col[:, 0]
    tile_counts = tile_count[:, 0]
    live_mask = jnp.arange(slot_count, dtype=jnp.int32)[None, :] < tile_counts[:, None]
    masked = adj_set * live_mask[:, :, None, None].astype(adj_set.dtype)
    part_rows = lax.all_gather(features, "rep", axis=0, tiled=True)
    col_blocks = part_rows.reshape(-1, tile_size, hidden_width)
    chosen = col_blocks[tile_cols]
    partial_value = jnp.einsum("bkij,bkjh->bih", masked, chosen, preferred_element_type=jnp.float32)
    part_sums = partial_value.astype(jnp.bfloat16).reshape(-1, hidden_width)
    aggregated = lax.psum_scatter(
        part_sums.astype(jnp.float32).astype(jnp.bfloat16), "node", scatter_dimension=0, tiled=True
    )
    preact = jnp.dot(aggregated, weight, preferred_element_type=jnp.float32) + bias
    node_out = jax.nn.silu(preact).astype(jnp.bfloat16)
    cotangent = out_grad[0].astype(jnp.float32)
    sigma = jax.nn.sigmoid(preact)
    pre_grad = (cotangent * sigma * (1.0 + preact * (1.0 - sigma))).astype(jnp.bfloat16)
    weight_terms = jnp.dot(aggregated.T, pre_grad, preferred_element_type=jnp.float32)
    weight_part = lax.psum_scatter(weight_terms, "rep", scatter_dimension=0, tiled=True)
    upstream = jnp.dot(pre_grad, weight.T, preferred_element_type=jnp.float32).astype(jnp.bfloat16)
    up_rows = lax.all_gather(upstream, "node", axis=0, tiled=True)
    up_blocks = up_rows.reshape(-1, tile_size, hidden_width)
    grad_total = jnp.zeros(col_blocks.shape, jnp.float32)
    for slot_index in range(slot_count):
        term = jnp.einsum(
            "bij,bih->bjh", masked[:, slot_index], up_blocks, preferred_element_type=jnp.float32
        )
        grad_total = grad_total.at[tile_cols[:, slot_index]].add(term)
    grad_terms = grad_total.reshape(-1, hidden_width)
    grad_rows = lax.psum_scatter(grad_terms, "rep", scatter_dimension=0, tiled=True)
    node_total = rows_dev * node_parts * rep_size
    weight_grad = lax.psum(weight_part, "node") * float(node_total) ** (-0.5)
    input_grad = grad_rows.astype(jnp.bfloat16)
    return (node_out.reshape(1, rows_dev, hidden_width), weight_grad, input_grad)


def solution(mesh):
    return jax.shard_map(
        on_device,
        mesh=mesh,
        in_specs=(
            P(("node", "rep"), None),
            P("rep", "node", None, None, None),
            P("rep", "node", None),
            P("rep", "node"),
            P(),
            P(),
            P("rep", "node", None),
        ),
        out_specs=(P("rep", "node", None), P("rep", None), P(("node", "rep"), None)),
        check_vma=False,
    )
```

profile of v0, /device:TPU:25, one launch (start us, length us, event | category | flops | bytes accessed | tf_op | source)
XLA Modules:
  0.0 233.4 jit_solution(6883140533739018445)
XLA Ops:
  7.2 0.0 reduce-scatter.4.cloned.1.call-start
  7.9 22.3 %all_gather.6 = bf16[256,512]{1,0:T(8,128)(2,1)S(1)} all-gather(bf16[32,512]{1,0:T(8,128)(2,1)} %param.19), channel_id=1, replica_groups=mesh['node'=4,'rep'=8] {'rep'}, dimensions={0}, use_global_device_ids=true | all-gather | bytes 294912 | tf_op jit(solution)/shard_map/all_gather | solution.py:18
  30.2 0.6 gather_fusion
  30.8 0.3 copy-done.2
  31.2 1.0 fusion.17
  32.1 0.0 reduce-scatter.4.cloned.1.call-update
  32.2 0.0 reduce-scatter.6.cloned.1.call-start
  32.2 0.6 fusion.26
  36.5 24.7 %reduce-scatter.4.cloned.1.call-done = bf16[32,512]{1,0:T(8,128)(2,1)} async-done(((bf16[128,512]{1,0:T(8,128)(2,1)}), bf16[32,512]{1,0:T(8,128)(2,1)}) %reduce-scatter.4.cloned.1.call-update) | async-done | bytes 32784 | tf_op jit(solution)/shard_map/reduce_scatter | solution.py:23
  61.2 1.0 convolution_add_fusion
  62.2 1.3 fusion.24
  63.6 0.0 reduce-scatter.8.cloned.1.call-start
  63.6 0.6 copy-done.7
  64.2 0.8 and_reduce_fusion.2
  72.6 0.8 and_reduce_fusion
  73.4 0.1 bitcast_multiply_fusion
  73.5 0.2 convolution_convert_fusion
  73.7 6.4 %all_gather.7 = bf16[128,512]{1,0:T(8,128)(2,1)S(1)} all-gather(bf16[32,512]{1,0:T(8,128)(2,1)S(1)} %convolution_convert_fusion), channel_id=1, replica_groups=mesh['node'=4,'rep'=8] {'node'}, dimensions={0}, use_global_device_ids=true | all-gather | bytes 163840 | tf_op jit(solution)/shard_map/all_gather | solution.py:34
  80.2 0.8 fusion.1
  81.0 0.8 fusion.4
  81.9 0.8 fusion.7
  82.7 0.8 fusion.10
  83.6 0.9 fusion.13
  84.5 0.8 fusion.16
  85.3 0.8 copy-done.1
  86.1 0.0 all-reduce.2.cloned.1.call-start
  86.2 40.4 %reduce-scatter.6.cloned.1.call-done = f32[64,512]{1,0:T(8,128)} async-done(((f32[512,512]{1,0:T(8,128)}), f32[64,512]{1,0:T(8,128)}) %reduce-scatter.6.cloned.1.call-update) | async-done | bytes 131088 | tf_op jit(solution)/shard_map/reduce_scatter | solution.py:32
  126.6 0.6 fusion.21
  127.2 63.3 %reduce-scatter.8.cloned.1.call-done = f32[32,512]{1,0:T(8,128)} async-done(((f32[256,512]{1,0:T(8,128)}), f32[32,512]{1,0:T(8,128)}) %reduce-scatter.8.cloned.1.call-update) | async-done | bytes 65552 | tf_op jit(solution)/shard_map/reduce_scatter | solution.py:43
  190.6 1.5 convert_element_type.39
  192.0 33.3 %all-reduce.2.cloned.1.call-done = f32[64,512]{1,0:T(8,128)} async-done(((f32[64,512]{1,0:T(8,128)}), f32[64,512]{1,0:T(8,128)}) %all-reduce.2.cloned.1.call-update) | async-done | bytes 131088 | tf_op jit(solution)/shard_map/psum | solution.py:45
  225.3 1.6 broadcast_multiply_fusion
  (20 shorter events, 0.2 us)
Async XLA Ops:
  7.2 54.0 %copy-start = (bf16[512,512]{1,0:T(8,128)(2,1)S(1)}, bf16[512,512]{1,0:T(8,128)(2,1)}, u32[]{:S(2)}) copy-start(bf16[512,512]{1,0:T(8,128)(2,1)} %param.23) | copy-start | bytes 1572868
  7.2 54.0 %reduce-scatter.4.cloned.1.call-start = ((), (), s32[]{:S(2)}) async-start(), calls=%async_computation.3 | async-start | bytes 163840 | tf_op jit(solution)/shard_map/reduce_scatter | solution.py:23
  7.9 22.3 %copy-start.5 = (s32[1,1,6]{2,1,0:T(1,128)S(1)}, s32[1,1,6]{2,1,0:T(1,128)}, u32[]{:S(2)}) copy-start(s32[1,1,6]{2,1,0:T(1,128)} %param.21) | copy-start | bytes 76
  30.2 0.9 copy-start.2
  32.2 94.4 %reduce-scatter.6.cloned.1.call-start = ((), (), s32[]{:S(2)}) async-start(), calls=%async_computation.4 | async-start | bytes 1179648 | tf_op jit(solution)/shard_map/reduce_scatter | solution.py:32
  35.2 25.9 %copy-start.6 = (f32[512]{0:T(512)S(1)}, f32[512]{0:T(512)}, u32[]{:S(2)}) copy-start(f32[512]{0:T(512)} %param.24) | copy-start | bytes 6148
  36.4 25.8 %copy-start.4 = (bf16[1,32,512]{2,1,0:T(8,128)(2,1)S(1)}, bf16[1,32,512]{2,1,0:T(8,128)(2,1)}, u32[]{:S(2)}) copy-start(bf16[1,32,512]{2,1,0:T(8,128)(2,1)} %param.25) | copy-start | bytes 98308
  61.2 1.0 copy-start.3
  63.5 0.7 copy-start.7
  63.6 127.0 %reduce-scatter.8.cloned.1.call-start = ((), (), s32[]{:S(2)}) async-start(), calls=%async_computation.6 | async-start | bytes 589824 | tf_op jit(solution)/shard_map/reduce_scatter | solution.py:43
  85.3 0.8 copy-start.1
  86.1 139.2 %all-reduce.2.cloned.1.call-start = ((), (), s32[]{:S(2)}) async-start(), calls=%async_computation.5 | async-start | bytes 262144 | tf_op jit(solution)/shard_map/psum | solution.py:45
Sparse Core Ops, SparseCore 0:
  32.3 28.8 reduce-scatter.3
  65.0 61.5 reduce-scatter.5
  129.9 60.6 reduce-scatter.7
  192.8 32.4 all-reduce.1
where the time goes:
time: 237 us; the launch traced here: 233 us
  waiting for transfers between devices  162 us (68%)
  blocking collectives  28.7 us (12%)
  between operations  25.8 us (11%)
  matrix products  8.55 us (4%)
  other arithmetic  5.36 us (2%)
  local copies, waits for them, and re-layouts  3.02 us (1%)
    reduce_scatter x1, waiting for transfers between devices, on_device(): lax.psum_scatter(grad_terms, 'rep', scatter_dimension=0, tiled=True)  63.3 us
    reduce_scatter x1, waiting for transfers between devices, on_device(): lax.psum_scatter(weight_terms, 'rep', scatter_dimension=0, tiled=True)  40.4 us
    psum x1, waiting for transfers between devices, on_device(): weight_grad = lax.psum(weight_part, 'node') * float(node_total) ** (-0.5)  33.3 us
    reduce_scatter x1, waiting for transfers between devices, on_device(): lax.psum_scatter(part_sums.astype(jnp.float32).astype(jnp.bfloat16), 'nod...  24.7 us
    all_gather x1, blocking collectives, on_device(): part_rows = lax.all_gather(features, 'rep', axis=0, tiled=True)  22.3 us
    all_gather x1, blocking collectives, on_device(): up_rows = lax.all_gather(upstream, 'node', axis=0, tiled=True)  6.41 us
    dot_general x6, matrix products, on_device(): jnp.einsum('bij,bih->bjh', masked[:, slot_index], up_blocks, preferred_el...  5.01 us
  transfers between devices with their start and end apart: 4, of which 4 were waited for; matrix products, arithmetic and copies ran while one was open for 4% of the time, Pallas kernels for 0%

commit v1 on v0

v1 whole, which is shorter than its diff:
```python
import functools

import jax
import jax.numpy as jnp
from jax import lax
from jax.experimental import pallas as pl
from jax.experimental.pallas import tpu as pltpu
from jax.sharding import PartitionSpec as P

LANES = 128
F32 = jnp.float32
BF16 = jnp.bfloat16
MESH = pl.DeviceIdType.MESH


def each(start, stop, body):
    if stop - start <= 8:
        for i in range(start, stop):
            body(i)
    else:
        def step(i, carry):
            body(i)
            return carry
        lax.fori_loop(start, stop, step, 0)


def kernel(
    n_node, n_rep, scale,
    cols, counts, feat, adj, weight, bias, out_grad,
    node_out, weight_grad, input_grad,
    feat_all, adj_v, dense, dense_t, w_v, og_v, sums, sums_in, agg_all, pg_all, no_v,
    wg_out, wg_in, wg_fin, wg_v, ig_out, ig_in, ig_v,
    local_sem, f_send, f_recv, s_send, s_recv, a_send, a_recv, p_send, p_recv,
    w_send, w_recv, i_send, i_recv, v_send, v_recv,
):
    s = lax.axis_index("node")
    r = lax.axis_index("rep")
    row_blocks, slots, tile, _ = adj_v.shape
    rows, width = feat.shape
    part_blocks = n_rep * rows // tile
    per_block = tile // rows
    splits = width // LANES
    groups = n_node // splits

    def node_peer(d):
        return lax.rem(s + d, n_node)

    def rep_peer(d):
        return lax.rem(r + d, n_rep)

    def send(axis, peer, src, dst, send_sems, recv_sems, d):
        return pltpu.make_async_remote_copy(
            src_ref=src, dst_ref=dst, send_sem=send_sems.at[d], recv_sem=recv_sems.at[d],
            device_id={axis: peer}, device_id_type=MESH,
        )

    loads = [
        pltpu.make_async_copy(src, dst, local_sem.at[i])
        for i, (src, dst) in enumerate(
            [(feat, feat_all.at[r]), (adj, adj_v), (weight, w_v), (out_grad, og_v)]
        )
    ]
    for load in loads:
        load.start()

    barrier = pltpu.get_barrier_semaphore()
    each(1, n_rep, lambda d: pl.semaphore_signal(barrier, inc=1, device_id={"rep": rep_peer(d)}, device_id_type=MESH))
    each(1, n_node, lambda d: pl.semaphore_signal(barrier, inc=1, device_id={"node": node_peer(d)}, device_id_type=MESH))
    pl.semaphore_wait(barrier, n_rep + n_node - 2)

    def feat_copy(d):
        return send("rep", rep_peer(d), feat, feat_all.at[r], f_send, f_recv, d)
    each(1, n_rep, lambda d: feat_copy(d).start())

    loads[1].wait()
    for b in range(row_blocks):
        def column(c, b=b):
            total = jnp.zeros((tile, tile), F32)
            for k in range(slots):
                live = jnp.logical_and(k < counts[b], cols[b, k] == c)
                total = total + adj_v[b, k].astype(F32) * jnp.where(live, 1.0, 0.0).astype(F32)
            at = pl.ds(pl.multiple_of(c * tile, tile), tile)
            dense[b, :, at] = total.astype(BF16)
            dense_t[b, at, :] = total.T.astype(BF16)
        each(0, part_blocks, column)
    loads[0].wait()
    loads[2].wait()
    loads[3].wait()
    each(1, n_rep, lambda d: feat_copy(d).wait_recv())

    part = feat_all[...].reshape(n_rep * rows, width)
    for b in range(row_blocks):
        value = jnp.dot(dense[b], part, preferred_element_type=F32).astype(BF16)
        sums[b * per_block:(b + 1) * per_block] = value.reshape(per_block, rows, width)

    def sum_copy(d):
        return send("node", node_peer(d), sums.at[node_peer(d)], sums_in.at[s], s_send, s_recv, d)
    each(1, n_node, lambda d: sum_copy(d).start())
    total = sums[s].astype(F32)
    for d in range(1, n_node):
        sum_copy(d).wait_recv()
        total = total + sums_in[lax.rem(s + n_node - d, n_node)].astype(F32)
    agg = total.astype(BF16)
    agg_all[s] = agg

    def agg_copy(d):
        return send("node", node_peer(d), agg_all.at[s], agg_all.at[s], a_send, a_recv, d)
    each(1, n_node, lambda d: agg_copy(d).start())

    preact = jnp.dot(agg, w_v[...], preferred_element_type=F32) + bias[...]
    sigma = lax.logistic(preact)
    pg_all[s] = (og_v[...].astype(F32) * sigma * (1.0 + preact * (1.0 - sigma))).astype(BF16)

    def pg_copy(d):
        return send("node", node_peer(d), pg_all.at[s], pg_all.at[s], p_send, p_recv, d)
    each(1, n_node, lambda d: pg_copy(d).start())
    no_v[...] = (preact * sigma).astype(BF16)
    store_no = pltpu.make_async_copy(no_v, node_out, local_sem.at[4])
    store_no.start()
    each(1, n_node, lambda d: agg_copy(d).wait_recv())
    each(1, n_node, lambda d: pg_copy(d).wait_recv())

    take = pl.ds(lax.div(s, splits) * splits, splits)
    agg_rows = agg_all[take].reshape(splits * rows, width)
    pg_cols = pg_all[take, :, pl.ds(pl.multiple_of(lax.rem(s, splits) * LANES, LANES), LANES)]
    terms = lax.dot_general(
        agg_rows, pg_cols.reshape(splits * rows, LANES), (((0,), (0,)), ((), ())), preferred_element_type=F32
    )
    wg_out[...] = terms.reshape(wg_out.shape).astype(wg_out.dtype)

    def wg_copy(d):
        return send("rep", rep_peer(d), wg_out.at[rep_peer(d)], wg_in.at[r], w_send, w_recv, d)
    each(1, n_rep, lambda d: wg_copy(d).start())

    upstream = lax.dot_general(
        pg_all[...].reshape(n_node * rows, width), w_v[...], (((1,), (1,)), ((), ())), preferred_element_type=F32
    ).astype(BF16)
    grad = jnp.dot(dense_t[0], upstream[:tile], preferred_element_type=F32)
    for b in range(1, row_blocks):
        grad = grad + jnp.dot(dense_t[b], upstream[b * tile:(b + 1) * tile], preferred_element_type=F32)
    ig_out[...] = grad.reshape(ig_out.shape).astype(BF16)

    def ig_copy(d):
        return send("rep", rep_peer(d), ig_out.at[rep_peer(d)], ig_in.at[r], i_send, i_recv, d)
    each(1, n_rep, lambda d: ig_copy(d).start())

    each(1, n_rep, lambda d: wg_copy(d).wait_recv())
    wg_in[r] = wg_out[r]
    total = jnp.sum(wg_in[...].astype(F32), axis=0)
    wg_fin[s] = (total * scale).astype(wg_fin.dtype)

    def fin_copy(d):
        return send("node", node_peer(d), wg_fin.at[s], wg_fin.at[s], v_send, v_recv, d)
    each(1, n_node, lambda d: fin_copy(d).start())

    each(1, n_rep, lambda d: ig_copy(d).wait_recv())
    ig_in[r] = ig_out[r]
    ig_v[...] = jnp.sum(ig_in[...].astype(F32), axis=0).astype(BF16)
    store_ig = pltpu.make_async_copy(ig_v, input_grad, local_sem.at[5])
    store_ig.start()

    each(1, n_node, lambda d: fin_copy(d).wait_recv())
    for c in range(splits):
        total = wg_fin[c].astype(F32)
        for g in range(1, groups):
            total = total + wg_fin[g * splits + c].astype(F32)
        wg_v[:, c * LANES:(c + 1) * LANES] = total
    store_wg = pltpu.make_async_copy(wg_v, weight_grad, local_sem.at[6])
    store_wg.start()

    for copy in (feat_copy, wg_copy, ig_copy):
        each(1, n_rep, lambda d: copy(d).wait_send())
    for copy in (sum_copy, agg_copy, pg_copy, fin_copy):
        each(1, n_node, lambda d: copy(d).wait_send())
    store_no.wait()
    store_ig.wait()
    store_wg.wait()


def on_device(features, adj_tiles, tile_col, tile_count, weight, bias, out_grad):
    n_node = lax.axis_size("node")
    n_rep = lax.axis_size("rep")
    rows, width = features.shape
    row_blocks, _, slots, tile, _ = adj_tiles.shape
    part_rows = n_rep * rows
    group_rows = n_node * rows
    assert group_rows == row_blocks * tile and part_rows % tile == 0 and tile % rows == 0
    assert width % LANES == 0 and n_node % (width // LANES) == 0
    w_rows = width // n_rep
    w_type = BF16 if w_rows % 16 == 0 else F32
    vmem = pl.BlockSpec(memory_space=pltpu.VMEM)
    smem = pl.BlockSpec(memory_space=pltpu.SMEM)
    hbm = pl.BlockSpec(memory_space=pl.ANY)
    dma = pltpu.SemaphoreType.DMA
    node_out, weight_grad, input_grad = pl.pallas_call(
        functools.partial(kernel, n_node, n_rep, float(part_rows * n_node) ** -0.5),
        out_shape=(
            jax.ShapeDtypeStruct((rows, width), BF16),
            jax.ShapeDtypeStruct((w_rows, width), F32),
            jax.ShapeDtypeStruct((rows, width), BF16),
        ),
        in_specs=[smem, smem, hbm, hbm, hbm, vmem, hbm],
        out_specs=(hbm, hbm, hbm),
        scratch_shapes=[
            pltpu.VMEM((n_rep, rows, width), BF16),
            pltpu.VMEM((row_blocks, slots, tile, tile), BF16),
            pltpu.VMEM((row_blocks, tile, part_rows), BF16),
            pltpu.VMEM((row_blocks, part_rows, tile), BF16),
            pltpu.VMEM((width, width), BF16),
            pltpu.VMEM((rows, width), BF16),
            pltpu.VMEM((n_node, rows, width), BF16),
            pltpu.VMEM((n_node, rows, width), BF16),
            pltpu.VMEM((n_node, rows, width), BF16),
            pltpu.VMEM((n_node, rows, width), BF16),
            pltpu.VMEM((rows, width), BF16),
            pltpu.VMEM((n_rep, w_rows, LANES), w_type),
            pltpu.VMEM((n_rep, w_rows, LANES), w_type),
            pltpu.VMEM((n_node, w_rows, LANES), w_type),
            pltpu.VMEM((w_rows, width), F32),
            pltpu.VMEM((n_rep, rows, width), BF16),
            pltpu.VMEM((n_rep, rows, width), BF16),
            pltpu.VMEM((rows, width), BF16),
            dma((7,)),
            dma((n_rep,)), dma((n_rep,)),
            dma((n_node,)), dma((n_node,)),
            dma((n_node,)), dma((n_node,)),
            dma((n_node,)), dma((n_node,)),
            dma((n_rep,)), dma((n_rep,)),
            dma((n_rep,)), dma((n_rep,)),
            dma((n_node,)), dma((n_node,)),
        ],
        compiler_params=pltpu.CompilerParams(
            collective_id=0, has_side_effects=True, vmem_limit_bytes=40 * 1024 * 1024
        ),
    )(
        tile_col[:, 0], tile_count[:, 0], features, adj_tiles[:, 0], weight, bias.reshape(1, width), out_grad[0]
    )
    return node_out[None], weight_grad, input_grad


def solution(mesh):
    return jax.shard_map(
        on_device,
        mesh=mesh,
        in_specs=(
            P(("node", "rep"), None),
            P("rep", "node", None, None, None),
            P("rep", "node", None),
            P("rep", "node"),
            P(),
            P(),
            P("rep", "node", None),
        ),
        out_specs=(P("rep", "node", None), P("rep", None), P(("node", "rep"), None)),
        check_vma=False,
    )
```

time: 237 us -> 38.5 us (0.16)
  the two profiles are of different devices: /device:TPU:25 before, /device:TPU:0 now
where the time goes in v1:
time: 38.5 us; the launch traced here: 38.2 us
  Pallas kernels  30.8 us (80%)
  local copies, waits for them, and re-layouts  6.04 us (16%)
  between operations  1.31 us (3%)
    pallas_call x1, Pallas kernels, on_device(): pl.pallas_call(functools.partial(kernel, n_node, n_rep, float(part_rows *...  30.8 us
    unnamed x15, local copies, waits for them, and re-layouts  6.04 us

profile of v1, /device:TPU:0, one launch (start us, length us, event | category | flops | bytes accessed | tf_op | source)
XLA Modules:
  0.0 38.2 jit_solution(915570048784631897)
XLA Ops:
  1.3 0.0 copy-start.4
  1.3 0.0 copy-start.5
  1.3 0.7 %copy-done.4 = f32[512]{0:T(512)S(1)} copy-done((f32[512]{0:T(512)S(1)}, f32[512]{0:T(512)}, u32[]{:S(2)}) %copy-start.4) | copy-done | bytes 2072
  2.0 0.0 copy-done.5
  2.0 0.0 copy-start
  2.0 1.0 %copy-done = bf16[512,512]{1,0:T(8,128)(2,1)S(1)} copy-done((bf16[512,512]{1,0:T(8,128)(2,1)S(1)}, bf16[512,512]{1,0:T(8,128)(2,1)}, u32[]{:S(2)}) %copy-start) | copy-done | bytes 524312
  3.0 0.0 copy-start.1
  3.0 0.9 %copy-done.1 = bf16[1,1,6,128,128]{4,3,2,1,0:T(8,128)(2,1)S(1)} copy-done((bf16[1,1,6,128,128]{4,3,2,1,0:T(8,128)(2,1)S(1)}, bf16[1,1,6,128,128]{4,3,2,1,0:T(8,128)(2,1)}, u32[]{:S(2)}) %copy-start.1) | copy-done | bytes 196632
  3.9 0.0 copy-start.2
  3.9 0.8 %copy-done.2 = bf16[32,512]{1,0:T(8,128)(2,1)S(1)} copy-done((bf16[32,512]{1,0:T(8,128)(2,1)S(1)}, bf16[32,512]{1,0:T(8,128)(2,1)}, u32[]{:S(2)}) %copy-start.2) | copy-done | bytes 32792
  4.7 0.0 copy-start.3
  4.7 0.8 %copy-done.3 = bf16[1,32,512]{2,1,0:T(8,128)(2,1)S(1)} copy-done((bf16[1,32,512]{2,1,0:T(8,128)(2,1)S(1)}, bf16[1,32,512]{2,1,0:T(8,128)(2,1)}, u32[]{:S(2)}) %copy-start.3) | copy-done | bytes 32792
  5.4 30.8 %shard_map.94 = (bf16[32,512]{1,0:T(8,128)(2,1)S(1)}, f32[64,512]{1,0:T(8,128)S(1)}, bf16[32,512]{1,0:T(8,128)(2,1)S(1)}) custom-call(s32[1,6]{1,0:T(1,128)S(1)} %bitcast.11, s32[1]{0:T(128)} %bitcast.6.counts, bf16[32,512]{1,0:T(8,128)(2,1)S(1)} %copy-done.2, bf16[1,6,128,128]{3,2,1,0:T(8,128)(2,1)S(1)} %bitcast.7, bf16[512,512]{1,0:T(8,128)(2,1)S(1)} %copy-done, ...), custom_call_target="tpu_custom_call" | custom-call | tf_op jit(solution)/shard_map/pallas_call | solution.py:195
  36.3 0.6 %copy.14 = bf16[1,32,512]{2,1,0:T(8,128)(2,1)} copy(bf16[1,32,512]{2,1,0:T(8,128)(2,1)S(1)} %bitcast.9) | data formatting | bytes 65536
  36.9 0.7 %copy.15 = f32[64,512]{1,0:T(8,128)} copy(f32[64,512]{1,0:T(8,128)S(1)} %get-tuple-element.13) | data formatting | bytes 262144
  37.6 0.6 %copy.16 = bf16[32,512]{1,0:T(8,128)(2,1)} copy(bf16[32,512]{1,0:T(8,128)(2,1)S(1)} %get-tuple-element.14) | data formatting | bytes 65536
Async XLA Ops:
  1.3 0.7 %copy-start.4 = (f32[512]{0:T(512)S(1)}, f32[512]{0:T(512)}, u32[]{:S(2)}) copy-start(f32[512]{0:T(512)} %param.12) | copy-start | bytes 6148
  1.3 0.7 %copy-start.5 = (s32[1,1,6]{2,1,0:T(1,128)S(1)}, s32[1,1,6]{2,1,0:T(1,128)}, u32[]{:S(2)}) copy-start(s32[1,1,6]{2,1,0:T(1,128)} %param.9) | copy-start | bytes 76
  2.0 1.0 %copy-start = (bf16[512,512]{1,0:T(8,128)(2,1)S(1)}, bf16[512,512]{1,0:T(8,128)(2,1)}, u32[]{:S(2)}) copy-start(bf16[512,512]{1,0:T(8,128)(2,1)} %weight.1) | copy-start | bytes 1572868
  3.0 0.9 %copy-start.1 = (bf16[1,1,6,128,128]{4,3,2,1,0:T(8,128)(2,1)S(1)}, bf16[1,1,6,128,128]{4,3,2,1,0:T(8,128)(2,1)}, u32[]{:S(2)}) copy-start(bf16[1,1,6,128,128]{4,3,2,1,0:T(8,128)(2,1)} %param.8) | copy-start | bytes 589828
  3.9 0.8 %copy-start.2 = (bf16[32,512]{1,0:T(8,128)(2,1)S(1)}, bf16[32,512]{1,0:T(8,128)(2,1)}, u32[]{:S(2)}) copy-start(bf16[32,512]{1,0:T(8,128)(2,1)} %feat.1) | copy-start | bytes 98308
  4.7 0.8 %copy-start.3 = (bf16[1,32,512]{2,1,0:T(8,128)(2,1)S(1)}, bf16[1,32,512]{2,1,0:T(8,128)(2,1)}, u32[]{:S(2)}) copy-start(bf16[1,32,512]{2,1,0:T(8,128)(2,1)} %param.13) | copy-start | bytes 98308

commit v2 on v1

v2 whole, which is shorter than its diff:
```python
import functools

import jax
import jax.numpy as jnp
from jax import lax
from jax.experimental import pallas as pl
from jax.experimental.pallas import tpu as pltpu
from jax.sharding import PartitionSpec as P

LANES = 128
F32 = jnp.float32
BF16 = jnp.bfloat16
MESH = pl.DeviceIdType.MESH
VMEM_GRANT = 63 * 1024 * 1024


def each(start, stop, body):
    if stop - start <= 8:
        for i in range(start, stop):
            body(i)
    else:
        def step(i, carry):
            body(i)
            return carry
        lax.fori_loop(start, stop, step, 0)


def kernel(
    n_node, n_rep, scale,
    cols, counts, feat, adj, weight, bias, out_grad,
    node_out, weight_grad, input_grad,
    feat_all, adj_v, dense, dense_t, w_v, bias_v, og_v, sums, sums_in, halves, agg_all, pg_all, no_v,
    wg_out, wg_in, wg_fin, wg_v, ig_out, ig_in, ig_v,
    local_sem, f_send, f_recv, w_send, w_recv, i_send, i_recv, o_send, o_recv, s_send, s_recv,
    c_send, c_recv, v_send, v_recv,
):
    s = lax.axis_index("node")
    r = lax.axis_index("rep")
    row_blocks, slots, tile, _ = adj_v.shape
    rows, width = feat.shape
    part_blocks = n_rep * rows // tile
    per_block = tile // rows
    splits = width // LANES
    groups = n_node // splits

    def node_peer(d):
        return lax.rem(s + d, n_node)

    node_half = n_node // 2
    core = lax.rem(s, 2)
    core_pair = s + 1 - 2 * core

    def rep_peer(d):
        return lax.rem(r + d, n_rep)

    def same_core(d):
        return lax.rem(s + 2 * d, n_node)

    def send(axis, peer, src, dst, send_sems, recv_sems, d):
        return pltpu.make_async_remote_copy(
            src_ref=src, dst_ref=dst, send_sem=send_sems.at[d], recv_sem=recv_sems.at[d],
            device_id={axis: peer}, device_id_type=MESH,
        )

    loads = [
        pltpu.make_async_copy(src, dst, local_sem.at[i])
        for i, (src, dst) in enumerate(
            [(feat, feat_all.at[r]), (adj, adj_v), (weight, w_v), (out_grad, og_v.at[lax.div(s, 2)]), (bias, bias_v)]
        )
    ]
    for load in loads:
        load.start()

    barrier = pltpu.get_barrier_semaphore()
    each(1, n_rep, lambda d: pl.semaphore_signal(barrier, inc=1, device_id={"rep": rep_peer(d)}, device_id_type=MESH))
    each(1, n_node, lambda d: pl.semaphore_signal(barrier, inc=1, device_id={"node": node_peer(d)}, device_id_type=MESH))
    pl.semaphore_wait(barrier, n_rep + n_node - 2)

    def feat_copy(d):
        return send("rep", rep_peer(d), feat, feat_all.at[r], f_send, f_recv, d)
    each(1, n_rep, lambda d: feat_copy(d).start())

    def og_copy(d):
        return send("node", same_core(d), out_grad, og_v.at[lax.div(s, 2)], o_send, o_recv, d)
    each(1, node_half, lambda d: og_copy(d).start())

    loads[1].wait()
    for b in range(row_blocks):
        def column(c, b=b):
            total = jnp.zeros((tile, tile), F32)
            for k in range(slots):
                live = jnp.logical_and(k < counts[b], cols[b, k] == c)
                total = total + adj_v[b, k].astype(F32) * jnp.where(live, 1.0, 0.0).astype(F32)
            at = pl.ds(pl.multiple_of(c * tile, tile), tile)
            dense[b, :, at] = total.astype(BF16)
            dense_t[b, at, :] = total.T.astype(BF16)
        each(0, part_blocks, column)
    loads[0].wait()
    loads[2].wait()
    loads[3].wait()
    loads[4].wait()
    each(1, n_rep, lambda d: feat_copy(d).wait_recv())

    part = feat_all[...].reshape(n_rep * rows, width)
    for b in range(row_blocks):
        value = jnp.dot(dense[b], part, preferred_element_type=F32).astype(BF16)
        value = value.reshape(per_block // 2, 2, rows, width)
        at = slice(b * per_block // 2, (b + 1) * per_block // 2)
        sums[0, at] = value[:, 0]
        sums[1, at] = value[:, 1]

    sum_copy = send("node", core_pair, sums.at[1 - core], sums_in, c_send, c_recv, 0)
    sum_copy.start()
    sum_copy.wait_recv()
    halves[lax.div(s, 2)] = (sums[core].astype(F32) + sums_in[...].astype(F32)).astype(BF16)

    def half_copy(d):
        at = halves.at[lax.div(s, 2)]
        return send("node", same_core(d), at, at, s_send, s_recv, d)
    each(1, node_half, lambda d: half_copy(d).start())
    each(1, node_half, lambda d: og_copy(d).wait_recv())
    each(1, node_half, lambda d: half_copy(d).wait_recv())
    agg = jnp.sum(halves[...].astype(F32), axis=0).astype(BF16)
    agg_all[core] = agg
    agg_copy = send("node", core_pair, agg_all.at[core], agg_all.at[core], c_send, c_recv, 1)
    agg_copy.start()

    preact = jnp.dot(agg.reshape(node_half * rows, width), w_v[...], preferred_element_type=F32) + bias_v[...]
    sigma = lax.logistic(preact)
    cotangent = og_v[...].reshape(node_half * rows, width).astype(F32)
    pre_grad = (cotangent * sigma * (1.0 + preact * (1.0 - sigma))).astype(BF16)
    pg_all[core] = pre_grad.reshape(node_half, rows, width)
    pg_copy = send("node", core_pair, pg_all.at[core], pg_all.at[core], c_send, c_recv, 2)
    pg_copy.start()
    no_v[...] = (preact * sigma).astype(BF16).reshape(node_half, rows, width)
    store_no = pltpu.make_async_copy(no_v.at[lax.div(s, 2)], node_out, local_sem.at[6])
    store_no.start()
    agg_copy.wait_recv()
    pg_copy.wait_recv()

    share = splits // 2
    take = pl.ds(lax.div(s, splits) * share, share)
    agg_rows = agg_all[:, take].reshape(splits * rows, width)
    pg_cols = pg_all[:, take, :, pl.ds(pl.multiple_of(lax.rem(s, splits) * LANES, LANES), LANES)]
    terms = lax.dot_general(
        agg_rows, pg_cols.reshape(splits * rows, LANES), (((0,), (0,)), ((), ())), preferred_element_type=F32
    )
    wg_out[...] = terms.reshape(wg_out.shape).astype(wg_out.dtype)

    def wg_copy(d):
        return send("rep", rep_peer(d), wg_out.at[rep_peer(d)], wg_in.at[r], w_send, w_recv, d)
    each(1, n_rep, lambda d: wg_copy(d).start())

    up = lax.dot_general(
        pg_all[...].reshape(n_node * rows, width), w_v[...], (((1,), (1,)), ((), ())), preferred_element_type=F32
    ).astype(BF16).reshape(2, node_half, rows, width)
    upstream = jnp.stack([up[i % 2, i // 2] for i in range(n_node)]).reshape(n_node * rows, width)
    grad = jnp.dot(dense_t[0], upstream[:tile], preferred_element_type=F32)
    for b in range(1, row_blocks):
        grad = grad + jnp.dot(dense_t[b], upstream[b * tile:(b + 1) * tile], preferred_element_type=F32)
    ig_out[...] = grad.reshape(ig_out.shape).astype(BF16)

    def ig_copy(d):
        return send("rep", rep_peer(d), ig_out.at[rep_peer(d)], ig_in.at[r], i_send, i_recv, d)
    each(1, n_rep, lambda d: ig_copy(d).start())

    each(1, n_rep, lambda d: wg_copy(d).wait_recv())
    wg_in[r] = wg_out[r]
    wg_fin[s] = (jnp.sum(wg_in[...].astype(F32), axis=0) * scale).astype(wg_fin.dtype)

    def fin_copy(d):
        return send("node", node_peer(d), wg_fin.at[s], wg_fin.at[s], v_send, v_recv, d)
    each(1, n_node, lambda d: fin_copy(d).start())

    each(1, n_rep, lambda d: ig_copy(d).wait_recv())
    ig_in[r] = ig_out[r]
    ig_v[...] = jnp.sum(ig_in[...].astype(F32), axis=0).astype(BF16)
    store_ig = pltpu.make_async_copy(ig_v, input_grad, local_sem.at[5])
    store_ig.start()

    each(1, n_node, lambda d: fin_copy(d).wait_recv())
    for c in range(splits):
        total = wg_fin[c].astype(F32)
        for g in range(1, groups):
            total = total + wg_fin[g * splits + c].astype(F32)
        wg_v[:, c * LANES:(c + 1) * LANES] = total
    store_wg = pltpu.make_async_copy(wg_v, weight_grad, local_sem.at[7])
    store_wg.start()

    for copy in (sum_copy, agg_copy, pg_copy):
        copy.wait_send()
    for copy in (feat_copy, wg_copy, ig_copy):
        each(1, n_rep, lambda d: copy(d).wait_send())
    for copy in (og_copy, half_copy):
        each(1, node_half, lambda d: copy(d).wait_send())
    each(1, n_node, lambda d: fin_copy(d).wait_send())
    store_no.wait()
    store_ig.wait()
    store_wg.wait()


def store_kernel(a, b, c, a_out, b_out, c_out, a_v, b_v, c_v, sems):
    moves = [(b, b_v, b_out), (a, a_v, a_out), (c, c_v, c_out)]
    loads = [pltpu.make_async_copy(src, mid, sems.at[i]) for i, (src, mid, _) in enumerate(moves)]
    stores = [pltpu.make_async_copy(mid, dst, sems.at[i + 3]) for i, (_, mid, dst) in enumerate(moves)]
    for load in loads:
        load.start()
    for load, copy in zip(loads, stores):
        load.wait()
        copy.start()
    for copy in stores:
        copy.wait()


def store(*arrays):
    hbm = pl.BlockSpec(memory_space=pl.ANY)
    return pl.pallas_call(
        store_kernel,
        out_shape=tuple(jax.ShapeDtypeStruct(a.shape, a.dtype) for a in arrays),
        in_specs=[hbm] * 3,
        out_specs=(hbm,) * 3,
        scratch_shapes=[*[pltpu.VMEM(a.shape, a.dtype) for a in arrays], pltpu.SemaphoreType.DMA((6,))],
        compiler_params=pltpu.CompilerParams(vmem_limit_bytes=VMEM_GRANT),
    )(*arrays)


def on_device(features, adj_tiles, tile_col, tile_count, weight, bias, out_grad):
    n_node = lax.axis_size("node")
    n_rep = lax.axis_size("rep")
    rows, width = features.shape
    row_blocks, _, slots, tile, _ = adj_tiles.shape
    part_rows = n_rep * rows
    group_rows = n_node * rows
    assert group_rows == row_blocks * tile and part_rows % tile == 0 and tile % rows == 0
    assert width % LANES == 0 and n_node % (width // LANES) == 0
    assert n_node % 2 == 0 and tile // rows % 2 == 0 and width // LANES % 2 == 0
    node_half = n_node // 2
    w_rows = width // n_rep
    w_type = BF16 if w_rows % 16 == 0 else F32
    smem = pl.BlockSpec(memory_space=pltpu.SMEM)
    hbm = pl.BlockSpec(memory_space=pl.ANY)
    dma = pltpu.SemaphoreType.DMA
    node_out, weight_grad, input_grad = pl.pallas_call(
        functools.partial(kernel, n_node, n_rep, float(part_rows * n_node) ** -0.5),
        out_shape=(
            jax.ShapeDtypeStruct((rows, width), BF16),
            jax.ShapeDtypeStruct((w_rows, width), F32),
            jax.ShapeDtypeStruct((rows, width), BF16),
        ),
        in_specs=[smem, smem] + [hbm] * 5,
        out_specs=(hbm, hbm, hbm),
        scratch_shapes=[
            pltpu.VMEM((n_rep, rows, width), BF16),
            pltpu.VMEM((row_blocks, slots, tile, tile), BF16),
            pltpu.VMEM((row_blocks, tile, part_rows), BF16),
            pltpu.VMEM((row_blocks, part_rows, tile), BF16),
            pltpu.VMEM((width, width), BF16),
            pltpu.VMEM((1, width), F32),
            pltpu.VMEM((node_half, rows, width), BF16),
            pltpu.VMEM((2, node_half, rows, width), BF16),
            pltpu.VMEM((node_half, rows, width), BF16),
            pltpu.VMEM((node_half, node_half, rows, width), BF16),
            pltpu.VMEM((2, node_half, rows, width), BF16),
            pltpu.VMEM((2, node_half, rows, width), BF16),
            pltpu.VMEM((node_half, rows, width), BF16),
            pltpu.VMEM((n_rep, w_rows, LANES), w_type),
            pltpu.VMEM((n_rep, w_rows, LANES), w_type),
            pltpu.VMEM((n_node, w_rows, LANES), w_type),
            pltpu.VMEM((w_rows, width), F32),
            pltpu.VMEM((n_rep, rows, width), BF16),
            pltpu.VMEM((n_rep, rows, width), BF16),
            pltpu.VMEM((rows, width), BF16),
            dma((8,)),
            *[dma((n_rep,))] * 6,
            *[dma((node_half,))] * 4,
            *[dma((3,))] * 2,
            *[dma((n_node,))] * 2,
        ],
        compiler_params=pltpu.CompilerParams(
            collective_id=0, has_side_effects=True, vmem_limit_bytes=VMEM_GRANT
        ),
    )(
        tile_col[:, 0], tile_count[:, 0], features, adj_tiles[:, 0], weight, bias.reshape(1, width), out_grad[0]
    )
    node_out, weight_grad, input_grad = store(node_out, weight_grad, input_grad)
    return node_out[None], weight_grad, input_grad


def solution(mesh):
    return jax.shard_map(
        on_device,
        mesh=mesh,
        in_specs=(
            P(("node", "rep"), None),
            P("rep", "node", None, None, None),
            P("rep", "node", None),
            P("rep", "node"),
            P(),
            P(),
            P("rep", "node", None),
        ),
        out_specs=(P("rep", "node", None), P("rep", None), P(("node", "rep"), None)),
        check_vma=False,
    )
```

time: 38.5 us -> 32.6 us (0.85)
  the two profiles are of different devices: /device:TPU:0 before, /device:TPU:25 now
where the time goes in v2:
time: 32.6 us; the launch traced here: 32.4 us
  Pallas kernels  31.1 us (95%)
  between operations  1.29 us (4%)
    pallas_call x1, Pallas kernels, on_device(): pl.pallas_call(functools.partial(kernel, n_node, n_rep, float(part_rows *...  29.5 us
    pallas_call x1, Pallas kernels, store(): pl.pallas_call(store_kernel, out_shape=tuple((jax.ShapeDtypeStruct(a.shap...  1.63 us

profile of v2, /device:TPU:25, one launch (start us, length us, event | category | flops | bytes accessed | tf_op | source)
XLA Modules:
  0.0 32.4 jit_solution(11119675623160712107)
XLA Ops:
  1.3 29.5 %shard_map.94 = (bf16[32,512]{1,0:T(8,128)(2,1)}, f32[64,512]{1,0:T(8,128)}, bf16[32,512]{1,0:T(8,128)(2,1)}) custom-call(s32[1,6]{1,0:T(1,128)} %bitcast.10, s32[1]{0:T(128)} %bitcast.6.counts, bf16[32,512]{1,0:T(8,128)(2,1)} %feat.1, bf16[1,6,128,128]{3,2,1,0:T(8,128)(2,1)} %bitcast.7, bf16[512,512]{1,0:T(8,128)(2,1)} %weight.1, f32[1,512]{1,0:T(1,128)} %bitcast.9, ...), custom_call_target="tpu_custom_call" | custom-call | tf_op jit(solution)/shard_map/pallas_call | solution.py:243
  30.8 1.6 %shard_map.95 = (bf16[32,512]{1,0:T(8,128)(2,1)}, f32[64,512]{1,0:T(8,128)}, bf16[32,512]{1,0:T(8,128)(2,1)}) custom-call(bf16[32,512]{1,0:T(8,128)(2,1)} %get-tuple-element.9.a, f32[64,512]{1,0:T(8,128)} %get-tuple-element.10.b, bf16[32,512]{1,0:T(8,128)(2,1)} %get-tuple-element.11.c), custom_call_target="tpu_custom_call" | custom-call | tf_op jit(solution)/shard_map/pallas_call | solution.py:217

commit v3 on v2

--- a/solution.py
+++ b/solution.py
@@ -11,7 +11,7 @@
 F32 = jnp.float32
 BF16 = jnp.bfloat16
 MESH = pl.DeviceIdType.MESH
-VMEM_GRANT = 63 * 1024 * 1024
+VMEM_GRANT = 40 * 1024 * 1024
 
 
 def each(start, stop, body):
@@ -27,9 +27,9 @@
 
 def kernel(
     n_node, n_rep, scale,
-    cols, counts, feat, adj, weight, bias, out_grad,
+    counts, cols_in, feat, adj, weight, bias, out_grad,
     node_out, weight_grad, input_grad,
-    feat_all, adj_v, dense, dense_t, w_v, bias_v, og_v, sums, sums_in, halves, agg_all, pg_all, no_v,
+    cols, feat_all, adj_v, dense, dense_t, w_v, bias_v, og_v, sums, sums_in, halves, agg_all, agg_t, pg_all, no_v,
     wg_out, wg_in, wg_fin, wg_v, ig_out, ig_in, ig_v,
     local_sem, f_send, f_recv, w_send, w_recv, i_send, i_recv, o_send, o_recv, s_send, s_recv,
     c_send, c_recv, v_send, v_recv,
@@ -65,7 +65,7 @@
     loads = [
         pltpu.make_async_copy(src, dst, local_sem.at[i])
         for i, (src, dst) in enumerate(
-            [(feat, feat_all.at[r]), (adj, adj_v), (weight, w_v), (out_grad, og_v.at[lax.div(s, 2)]), (bias, bias_v)]
+            [(feat, feat_all.at[r]), (adj, adj_v), (weight, w_v), (out_grad, og_v.at[lax.div(s, 2)]), (bias, bias_v), (cols_in, cols)]
         )
     ]
     for load in loads:
@@ -85,6 +85,7 @@
     each(1, node_half, lambda d: og_copy(d).start())
 
     loads[1].wait()
+    loads[5].wait()
     for b in range(row_blocks):
         def column(c, b=b):
             total = jnp.zeros((tile, tile), F32)
@@ -133,18 +134,16 @@
     pg_copy = send("node", core_pair, pg_all.at[core], pg_all.at[core], c_send, c_recv, 2)
     pg_copy.start()
     no_v[...] = (preact * sigma).astype(BF16).reshape(node_half, rows, width)
-    store_no = pltpu.make_async_copy(no_v.at[lax.div(s, 2)], node_out, local_sem.at[6])
+    store_no = pltpu.make_async_copy(no_v.at[lax.div(s, 2)], node_out, local_sem.at[8])
     store_no.start()
-    agg_copy.wait_recv()
-    pg_copy.wait_recv()
-
     share = splits // 2
     take = pl.ds(lax.div(s, splits) * share, share)
-    agg_rows = agg_all[:, take].reshape(splits * rows, width)
+    agg_copy.wait_recv()
+    agg_t[...] = agg_all[:, take].reshape(splits * rows, width).T
+    pg_copy.wait_recv()
+
     pg_cols = pg_all[:, take, :, pl.ds(pl.multiple_of(lax.rem(s, splits) * LANES, LANES), LANES)]
-    terms = lax.dot_general(
-        agg_rows, pg_cols.reshape(splits * rows, LANES), (((0,), (0,)), ((), ())), preferred_element_type=F32
-    )
+    terms = jnp.dot(agg_t[...], pg_cols.reshape(splits * rows, LANES), preferred_element_type=F32)
     wg_out[...] = terms.reshape(wg_out.shape).astype(wg_out.dtype)
 
     def wg_copy(d):
@@ -175,7 +174,7 @@
     each(1, n_rep, lambda d: ig_copy(d).wait_recv())
     ig_in[r] = ig_out[r]
     ig_v[...] = jnp.sum(ig_in[...].astype(F32), axis=0).astype(BF16)
-    store_ig = pltpu.make_async_copy(ig_v, input_grad, local_sem.at[5])
+    store_ig = pltpu.make_async_copy(ig_v, input_grad, local_sem.at[7])
     store_ig.start()
 
     each(1, n_node, lambda d: fin_copy(d).wait_recv())
@@ -184,7 +183,7 @@
         for g in range(1, groups):
             total = total + wg_fin[g * splits + c].astype(F32)
         wg_v[:, c * LANES:(c + 1) * LANES] = total
-    store_wg = pltpu.make_async_copy(wg_v, weight_grad, local_sem.at[7])
+    store_wg = pltpu.make_async_copy(wg_v, weight_grad, local_sem.at[9])
     store_wg.start()
 
     for copy in (sum_copy, agg_copy, pg_copy):
@@ -199,16 +198,13 @@
     store_wg.wait()
 
 
-def store_kernel(a, b, c, a_out, b_out, c_out, a_v, b_v, c_v, sems):
-    moves = [(b, b_v, b_out), (a, a_v, a_out), (c, c_v, c_out)]
-    loads = [pltpu.make_async_copy(src, mid, sems.at[i]) for i, (src, mid, _) in enumerate(moves)]
-    stores = [pltpu.make_async_copy(mid, dst, sems.at[i + 3]) for i, (_, mid, dst) in enumerate(moves)]
-    for load in loads:
-        load.start()
-    for load, copy in zip(loads, stores):
-        load.wait()
+def store_kernel(a, b, c, a_out, b_out, c_out, sems):
+    copies = [
+        pltpu.make_async_copy(src, dst, sems.at[i]) for i, (src, dst) in enumerate([(b, b_out), (a, a_out), (c, c_out)])
+    ]
+    for copy in copies:
         copy.start()
-    for copy in stores:
+    for copy in copies:
         copy.wait()
 
 
@@ -219,8 +215,8 @@
         out_shape=tuple(jax.ShapeDtypeStruct(a.shape, a.dtype) for a in arrays),
         in_specs=[hbm] * 3,
         out_specs=(hbm,) * 3,
-        scratch_shapes=[*[pltpu.VMEM(a.shape, a.dtype) for a in arrays], pltpu.SemaphoreType.DMA((6,))],
-        compiler_params=pltpu.CompilerParams(vmem_limit_bytes=VMEM_GRANT),
+        scratch_shapes=[pltpu.SemaphoreType.DMA((3,))],
+        compiler_params=pltpu.CompilerParams(vmem_limit_bytes=1024 * 1024),
     )(*arrays)
 
 
@@ -237,7 +233,6 @@
     node_half = n_node // 2
     w_rows = width // n_rep
     w_type = BF16 if w_rows % 16 == 0 else F32
-    smem = pl.BlockSpec(memory_space=pltpu.SMEM)
     hbm = pl.BlockSpec(memory_space=pl.ANY)
     dma = pltpu.SemaphoreType.DMA
     node_out, weight_grad, input_grad = pl.pallas_call(
@@ -247,9 +242,10 @@
             jax.ShapeDtypeStruct((w_rows, width), F32),
             jax.ShapeDtypeStruct((rows, width), BF16),
         ),
-        in_specs=[smem, smem] + [hbm] * 5,
+        in_specs=[pl.BlockSpec(memory_space=pltpu.SMEM)] + [hbm] * 6,
         out_specs=(hbm, hbm, hbm),
         scratch_shapes=[
+            pltpu.SMEM((row_blocks, slots), jnp.int32),
             pltpu.VMEM((n_rep, rows, width), BF16),
             pltpu.VMEM((row_blocks, slots, tile, tile), BF16),
             pltpu.VMEM((row_blocks, tile, part_rows), BF16),
@@ -261,6 +257,7 @@
             pltpu.VMEM((node_half, rows, width), BF16),
             pltpu.VMEM((node_half, node_half, rows, width), BF16),
             pltpu.VMEM((2, node_half, rows, width), BF16),
+            pltpu.VMEM((width, width // LANES * rows), BF16),
             pltpu.VMEM((2, node_half, rows, width), BF16),
             pltpu.VMEM((node_half, rows, width), BF16),
             pltpu.VMEM((n_rep, w_rows, LANES), w_type),
@@ -270,7 +267,7 @@
             pltpu.VMEM((n_rep, rows, width), BF16),
             pltpu.VMEM((n_rep, rows, width), BF16),
             pltpu.VMEM((rows, width), BF16),
-            dma((8,)),
+            dma((10,)),
             *[dma((n_rep,))] * 6,
             *[dma((node_half,))] * 4,
             *[dma((3,))] * 2,
@@ -280,7 +277,11 @@
             collective_id=0, has_side_effects=True, vmem_limit_bytes=VMEM_GRANT
         ),
     )(
-        tile_col[:, 0], tile_count[:, 0], features, adj_tiles[:, 0], weight, bias.reshape(1, width), out_grad[0]
+        tile_count[:, 0],
+        *[
+            pltpu.with_memory_space_constraint(x, pltpu.HBM)
+            for x in (tile_col[:, 0], features, adj_tiles[:, 0], weight, bias.reshape(1, width), out_grad[0])
+        ],
     )
     node_out, weight_grad, input_grad = store(node_out, weight_grad, input_grad)
     return node_out[None], weight_grad, input_grad

time: 32.6 us -> 30.6 us (0.939)
  Pallas kernels: 31.1 us -> 29.2 us
    pallas_call x1, Pallas kernels: 29.5 us -> 28.5 us  [on_device(): pl.pallas_call(functools.partial(kernel, n_node, n_rep, float(part_rows *...]
    pallas_call x1, Pallas kernels: 1.63 us -> 0.7 us  [store(): pl.pallas_call(store_kernel, out_shape=tuple((jax.ShapeDtypeStruct(a.shap...]
where the time goes in v3:
time: 30.6 us; the launch traced here: 30.5 us
  Pallas kernels  29.2 us (95%)
  between operations  1.29 us (4%)
    pallas_call x1, Pallas kernels, on_device(): pl.pallas_call(functools.partial(kernel, n_node, n_rep, float(part_rows *...  28.5 us
    pallas_call x1, Pallas kernels, store(): pl.pallas_call(store_kernel, out_shape=tuple((jax.ShapeDtypeStruct(a.shap...  0.7 us

profile of v3, /device:TPU:25, one launch (start us, length us, event | category | flops | bytes accessed | tf_op | source)
XLA Modules:
  0.0 30.5 jit_solution(10342671872343020159)
XLA Ops:
  1.3 28.5 %shard_map.94 = (bf16[32,512]{1,0:T(8,128)(2,1)S(1)}, f32[64,512]{1,0:T(8,128)S(1)}, bf16[32,512]{1,0:T(8,128)(2,1)S(1)}) custom-call(s32[1]{0:T(128)} %bitcast.6.counts, s32[1,6]{1,0:T(1,128)} %bitcast.10, bf16[32,512]{1,0:T(8,128)(2,1)} %feat.1, bf16[1,6,128,128]{3,2,1,0:T(8,128)(2,1)} %bitcast.7, bf16[512,512]{1,0:T(8,128)(2,1)} %weight.1, ...), custom_call_target="tpu_custom_call" | custom-call | tf_op jit(solution)/shard_map/pallas_call | solution.py:238
  29.8 0.7 %shard_map.95 = (bf16[32,512]{1,0:T(8,128)(2,1)}, f32[64,512]{1,0:T(8,128)}, bf16[32,512]{1,0:T(8,128)(2,1)}) custom-call(bf16[32,512]{1,0:T(8,128)(2,1)S(1)} %get-tuple-element.9.a, f32[64,512]{1,0:T(8,128)S(1)} %get-tuple-element.10.b, bf16[32,512]{1,0:T(8,128)(2,1)S(1)} %get-tuple-element.11.c), custom_call_target="tpu_custom_call" | custom-call | tf_op jit(solution)/shard_map/pallas_call | solution.py:213

commit v4 on v3

--- a/solution.py
+++ b/solution.py
@@ -62,6 +62,9 @@
             device_id={axis: peer}, device_id_type=MESH,
         )
 
+    barrier = pltpu.get_barrier_semaphore()
+    each(1, n_rep, lambda d: pl.semaphore_signal(barrier, inc=1, device_id={"rep": rep_peer(d)}, device_id_type=MESH))
+    each(1, n_node, lambda d: pl.semaphore_signal(barrier, inc=1, device_id={"node": node_peer(d)}, device_id_type=MESH))
     loads = [
         pltpu.make_async_copy(src, dst, local_sem.at[i])
         for i, (src, dst) in enumerate(
@@ -70,14 +73,11 @@
     ]
     for load in loads:
         load.start()
-
-    barrier = pltpu.get_barrier_semaphore()
-    each(1, n_rep, lambda d: pl.semaphore_signal(barrier, inc=1, device_id={"rep": rep_peer(d)}, device_id_type=MESH))
-    each(1, n_node, lambda d: pl.semaphore_signal(barrier, inc=1, device_id={"node": node_peer(d)}, device_id_type=MESH))
+    loads[0].wait()
     pl.semaphore_wait(barrier, n_rep + n_node - 2)
 
     def feat_copy(d):
-        return send("rep", rep_peer(d), feat, feat_all.at[r], f_send, f_recv, d)
+        return send("rep", rep_peer(d), feat_all.at[r], feat_all.at[r], f_send, f_recv, d)
     each(1, n_rep, lambda d: feat_copy(d).start())
 
     def og_copy(d):
@@ -96,7 +96,6 @@
             dense[b, :, at] = total.astype(BF16)
             dense_t[b, at, :] = total.T.astype(BF16)
         each(0, part_blocks, column)
-    loads[0].wait()
     loads[2].wait()
     loads[3].wait()
     loads[4].wait()

time: 30.6 us -> 30.3 us (level)
  no operation moved by 1% of the time
where the time goes in v4:
time: 30.3 us; the launch traced here: 30.2 us
  Pallas kernels  28.9 us (95%)
  between operations  1.29 us (4%)
    pallas_call x1, Pallas kernels, on_device(): pl.pallas_call(functools.partial(kernel, n_node, n_rep, float(part_rows *...  28.2 us
    pallas_call x1, Pallas kernels, store(): pl.pallas_call(store_kernel, out_shape=tuple((jax.ShapeDtypeStruct(a.shap...  0.7 us

profile of v4, /device:TPU:25, one launch (start us, length us, event | category | flops | bytes accessed | tf_op | source)
XLA Modules:
  0.0 30.2 jit_solution(3558944484451529932)
XLA Ops:
  1.3 28.2 %shard_map.94 = (bf16[32,512]{1,0:T(8,128)(2,1)S(1)}, f32[64,512]{1,0:T(8,128)S(1)}, bf16[32,512]{1,0:T(8,128)(2,1)S(1)}) custom-call(s32[1]{0:T(128)} %bitcast.6.counts, s32[1,6]{1,0:T(1,128)} %bitcast.10, bf16[32,512]{1,0:T(8,128)(2,1)} %feat.1, bf16[1,6,128,128]{3,2,1,0:T(8,128)(2,1)} %bitcast.7, bf16[512,512]{1,0:T(8,128)(2,1)} %weight.1, ...), custom_call_target="tpu_custom_call" | custom-call | tf_op jit(solution)/shard_map/pallas_call | solution.py:237
  29.5 0.7 %shard_map.95 = (bf16[32,512]{1,0:T(8,128)(2,1)}, f32[64,512]{1,0:T(8,128)}, bf16[32,512]{1,0:T(8,128)(2,1)}) custom-call(bf16[32,512]{1,0:T(8,128)(2,1)S(1)} %get-tuple-element.9.a, f32[64,512]{1,0:T(8,128)S(1)} %get-tuple-element.10.b, bf16[32,512]{1,0:T(8,128)(2,1)S(1)} %get-tuple-element.11.c), custom_call_target="tpu_custom_call" | custom-call | tf_op jit(solution)/shard_map/pallas_call | solution.py:212

commit v5 on v4

--- a/solution.py
+++ b/solution.py
@@ -162,17 +162,19 @@
         return send("rep", rep_peer(d), ig_out.at[rep_peer(d)], ig_in.at[r], i_send, i_recv, d)
     each(1, n_rep, lambda d: ig_copy(d).start())
 
-    each(1, n_rep, lambda d: wg_copy(d).wait_recv())
-    wg_in[r] = wg_out[r]
-    wg_fin[s] = (jnp.sum(wg_in[...].astype(F32), axis=0) * scale).astype(wg_fin.dtype)
+    def collect(copy, got, total):
+        def add(d, total):
+            copy(d).wait_recv()
+            return total + got[lax.rem(r + n_rep - d, n_rep)].astype(F32)
+        return lax.fori_loop(1, n_rep, add, total, unroll=n_rep <= 8)
+
+    wg_fin[s] = (collect(wg_copy, wg_in, wg_out[r].astype(F32)) * scale).astype(wg_fin.dtype)
 
     def fin_copy(d):
         return send("node", node_peer(d), wg_fin.at[s], wg_fin.at[s], v_send, v_recv, d)
     each(1, n_node, lambda d: fin_copy(d).start())
 
-    each(1, n_rep, lambda d: ig_copy(d).wait_recv())
-    ig_in[r] = ig_out[r]
-    ig_v[...] = jnp.sum(ig_in[...].astype(F32), axis=0).astype(BF16)
+    ig_v[...] = collect(ig_copy, ig_in, ig_out[r].astype(F32)).astype(BF16)
     store_ig = pltpu.make_async_copy(ig_v, input_grad, local_sem.at[7])
     store_ig.start()
 

time: 30.3 us -> 30.3 us (level)
  no operation moved by 1% of the time
where the time goes in v5:
time: 30.3 us; the launch traced here: 30.2 us
  Pallas kernels  28.9 us (95%)
  between operations  1.29 us (4%)
    pallas_call x1, Pallas kernels, on_device(): pl.pallas_call(functools.partial(kernel, n_node, n_rep, float(part_rows *...  28.2 us
    pallas_call x1, Pallas kernels, store(): pl.pallas_call(store_kernel, out_shape=tuple((jax.ShapeDtypeStruct(a.shap...  0.7 us

profile of v5, /device:TPU:25, one launch (start us, length us, event | category | flops | bytes accessed | tf_op | source)
XLA Modules:
  0.0 30.2 jit_solution(11213584846513718421)
XLA Ops:
  1.3 28.2 %shard_map.94 = (bf16[32,512]{1,0:T(8,128)(2,1)S(1)}, f32[64,512]{1,0:T(8,128)S(1)}, bf16[32,512]{1,0:T(8,128)(2,1)S(1)}) custom-call(s32[1]{0:T(128)} %bitcast.6.counts, s32[1,6]{1,0:T(1,128)} %bitcast.10, bf16[32,512]{1,0:T(8,128)(2,1)} %feat.1, bf16[1,6,128,128]{3,2,1,0:T(8,128)(2,1)} %bitcast.7, bf16[512,512]{1,0:T(8,128)(2,1)} %weight.1, ...), custom_call_target="tpu_custom_call" | custom-call | tf_op jit(solution)/shard_map/pallas_call | solution.py:239
  29.5 0.7 %shard_map.95 = (bf16[32,512]{1,0:T(8,128)(2,1)}, f32[64,512]{1,0:T(8,128)}, bf16[32,512]{1,0:T(8,128)(2,1)}) custom-call(bf16[32,512]{1,0:T(8,128)(2,1)S(1)} %get-tuple-element.9.a, f32[64,512]{1,0:T(8,128)S(1)} %get-tuple-element.10.b, bf16[32,512]{1,0:T(8,128)(2,1)S(1)} %get-tuple-element.11.c), custom_call_target="tpu_custom_call" | custom-call | tf_op jit(solution)/shard_map/pallas_call | solution.py:214
